TPU v7x, 32 devices: a whole 2x2x4 slice. The times are simulated.
32 devices in a mesh: dim: 4 (over y, core), rows: 8 (over z, x).
Axes of the slice: x: 2, y: 2, z: 4, core: 2. Of those that a mesh axis runs over, the one named last changes fastest.
Arguments:
- user_rows: bfloat16 [512, 1024], P('rows', 'dim'), may hold values from -0.1875 to 0.1875
- item_table: bfloat16 [8192, 1024], P('rows', 'dim')
- observed_items: int32 [512, 32], P('rows'), may hold values from 0 to 8191, as said below
- counts: int32 [512], P('rows'), may hold values from 1 to 32
- item_row: int32 [8192], replicated, may hold values from 0 to 8191, as said below
Outputs:
- new_users: float32 [512, 1024], P('rows', 'dim')
Inputs may be any that keep to these rules, and one draw needn't show every extreme that they name: item_row is a permutation; rows k * 1024 to (k + 1) * 1024 - 1 of item_table form item block k. In the rows of observed_items of each 64 consecutive users (padding slots included), exactly 256 slots name items whose table row lies in item block k, for every k.
All inputs are finite; a program needn't handle non-finite values.
Results may differ from a plain program's by a relative error of at most 0.0003.
Values may be sent and summed in bfloat16 or wider, within the bound.
A program may use at most 64 MiB of HBM per device.

v0:
```python
import jax
import jax.numpy as jnp
from jax import lax
from jax.sharding import PartitionSpec as P


def on_device(user_rows, item_table, observed_items, counts, item_row):
    highest = lax.Precision.HIGHEST
    width = user_rows.shape[1]
    users_dev = user_rows.shape[0]
    list_len = observed_items.shape[1]
    weight_unobs = 32.0 / item_row.shape[0]
    gram_part = lax.dot_general(
        item_table,
        lax.all_gather(item_table, "dim", axis=1, tiled=True),
        (((0,), (0,)), ((), ())),
        preferred_element_type=jnp.float32,
    )
    gram_rows = lax.psum(gram_part, "rows")
    gram_times = lax.dot_general(
        lax.all_gather(user_rows, "dim", axis=1, tiled=True).astype(jnp.float32),
        gram_rows,
        (((1,), (1,)), ((), ())),
        precision=highest,
    )
    table_rows = item_row[observed_items]
    shard_rows = lax.all_gather(item_table, "rows", axis=0, tiled=True)
    inside = (table_rows >= 0) & (table_rows < shard_rows.shape[0])
    picked = shard_rows[jnp.clip(table_rows, 0, shard_rows.shape[0] - 1)]
    fetched = jnp.where(
        inside[..., None], picked, jnp.zeros((users_dev, list_len, width), jnp.bfloat16)
    )
    partial_value = jnp.einsum("ub,ujb->uj", user_rows, fetched, preferred_element_type=jnp.float32)
    predicted = lax.psum(partial_value, "dim")
    live = (lax.broadcasted_iota(jnp.int32, (users_dev, list_len), 1) < counts[:, None]).astype(
        jnp.float32
    )
    residual = live * (predicted - 1.0)
    first_column = lax.axis_index("dim") * width
    diag_block = lax.dynamic_slice_in_dim(gram_rows, first_column, width, 1)
    diag_shift = weight_unobs * diag_block + jnp.eye(width, dtype=jnp.float32)
    own_float = user_rows.astype(jnp.float32)
    shift_factor = jnp.linalg.cholesky(diag_shift)
    shift_inverse = jax.scipy.linalg.cho_solve(
        (shift_factor, True), jnp.eye(width, dtype=jnp.float32)
    )
    masked = fetched.astype(jnp.float32) * live[..., None]
    gradient = (
        jnp.einsum("uj,ujb->ub", residual, masked, precision=highest)
        + weight_unobs * gram_times
        + own_float
    )
    scaled_grad = jnp.dot(gradient, shift_inverse, precision=highest)
    scaled_rows = jnp.einsum("ujb,bc->ujc", masked, shift_inverse, precision=highest)
    inner = jnp.einsum("ujb,ukb->ujk", scaled_rows, masked, precision=highest) + jnp.eye(
        list_len, dtype=jnp.float32
    )
    projected = jnp.einsum("ujb,ub->uj", masked, scaled_grad, precision=highest)
    inner_factor = jnp.linalg.cholesky(inner)
    middle = jax.scipy.linalg.solve_triangular(inner_factor, projected[..., None], lower=True)
    weights = jax.scipy.linalg.solve_triangular(inner_factor, middle, lower=True, trans="T")[..., 0]
    update = scaled_grad - jnp.einsum("uj,ujb->ub", weights, scaled_rows, precision=highest)
    return own_float - update


def solution(mesh):
    in_specs = (P("rows", "dim"), P("rows", "dim"), P("rows", None), P("rows"), P())
    out_specs = P("rows", "dim")
    return jax.shard_map(
        on_device, mesh=mesh, in_specs=in_specs, out_specs=out_specs, check_vma=False
    )
```

profile of v0, /device:TPU:12, one launch (start us, length us, event | category | flops | bytes accessed | tf_op | source)
XLA Modules:
  0.0 443.7 jit_solution(16750682667686303518)
XLA Ops:
  6.5 0.7 all-gather.5.cloned.1.call-update
  7.3 24.7 %all-gather.5.cloned.1.call-done = bf16[1024,1024]{1,0:T(8,128)(2,1)} async-done(((bf16[1024,256]{1,0:T(8,128)(2,1)}), bf16[1024,1024]{1,0:T(8,128)(2,1)}) %all-gather.5.cloned.1.call-update) | async-done | bytes 2097168 | tf_op jit(solution)/shard_map/all_gather | solution.py:15
  32.0 3.7 fusion.47
  36.7 11.8 %gather_fusion = s32[2048]{0:T(1024)S(1)} fusion(s32[8192]{0:T(1024)S(1)} %copy-done, s32[2048]{0:T(1024)S(1)} %broadcast_clamp_fusion.1), kind=kCustom, calls=%fused_computation | custom fusion | bytes 24576 | tf_op jit(solution)/shard_map/gather | solution.py:26
  48.7 5.9 %all_gather.11 = bf16[64,1024]{1,0:T(8,128)(2,1)} all-gather(bf16[64,256]{1,0:T(8,128)(2,1)S(1)} %copy-done.4), channel_id=1, replica_groups=mesh['dim'=4,'rows'=8] {'dim'}, dimensions={1}, use_global_device_ids=true | all-gather | bytes 163840 | tf_op jit(solution)/shard_map/all_gather | solution.py:21
  54.8 59.5 %all-reduce.3.cloned.1.call-done = f32[256,1024]{0,1:T(8,128)} async-done(((f32[256,1024]{0,1:T(8,128)}), f32[256,1024]{0,1:T(8,128)}) %all-reduce.3.cloned.1.call-update) | async-done | bytes 1048592 | tf_op jit(solution)/shard_map/psum | solution.py:19
  114.3 1.0 multiply_add_fusion
  115.4 1.0 fusion.21
  116.5 11.7 %cholesky.65 = f32[128,128]{1,0:T(8,128)S(1)} custom-call(f32[128,128]{1,0:T(8,128)S(1)} %cholesky.159), custom_call_target="Cholesky" | custom-call | tf_op jit(solution)/shard_map/jit(cholesky)/cholesky | solution.py:43
  128.2 9.8 %custom-call.29 = f32[1,128,128]{1,2,0:T(8,128)S(1)} custom-call(f32[1,128,128]{2,1,0:T(8,128)S(1)} %get-tuple-element.26), custom_call_target="InvertDiagBlocksLowerTriangular" | custom-call | tf_op jit(solution)/shard_map/jit(cholesky)/cholesky | solution.py:43
  138.5 11.7 %cholesky.135 = f32[128,128]{1,0:T(8,128)S(1)} custom-call(f32[128,128]{1,0:T(8,128)S(1)} %convolution_subtract_fusion.2), custom_call_target="Cholesky" | custom-call | tf_op jit(solution)/shard_map/jit(cholesky)/cholesky | solution.py:43
  150.3 0.7 compare_reduce_fusion.1
  152.4 4.2 while.1
  153.2 1.3 bitcast_dynamic-update-slice_fusion.2
  155.2 1.3 bitcast_dynamic-update-slice_fusion.2
  156.6 19.7 %custom-call.30 = f32[2,128,128]{1,2,0:T(8,128)S(1)} custom-call(f32[2,128,128]{2,1,0:T(8,128)S(1)} %get-tuple-element.12), custom_call_target="InvertDiagBlocksLowerTriangular" | custom-call | tf_op jit(solution)/shard_map/jit(_cho_solve)/triangular_solve | solution.py:44
  178.1 11.7 %all-gather.3.cloned.1.call-done = bf16[8192,256]{1,0:T(8,128)(2,1)} async-done(((bf16[1024,256]{1,0:T(8,128)(2,1)}), bf16[8192,256]{1,0:T(8,128)(2,1)}) %all-gather.3.cloned.1.call-update) | async-done | bytes 4194320 | tf_op jit(solution)/shard_map/all_gather | solution.py:27
  189.8 9.4 %gather_fusion.1 = bf16[2048,256]{1,0:T(8,128)(2,1)S(1)} fusion(bf16[8192,256]{1,0:T(8,128)(2,1)} %all-gather.3.cloned.1.call-done, s32[2048]{0:T(1024)S(1)} %broadcast_clamp_fusion), kind=kCustom, calls=%fused_computation.1 | custom fusion | bytes 2105344 | tf_op jit(solution)/shard_map/gather | solution.py:29
  199.6 10.4 %psum.14 = f32[64,32]{1,0:T(8,128)S(1)} all-reduce(f32[64,32]{1,0:T(8,128)S(1)} %bitcast.110), channel_id=1, replica_groups=mesh['dim'=4,'rows'=8] {'dim'}, use_global_device_ids=true, to_apply=%region_0.0 | all-reduce | flops 2048 | bytes 16384 | tf_op jit(solution)/shard_map/psum | solution.py:34
  210.2 1.7 fusion.3
  211.9 1.9 fusion.2
  215.2 2.4 fusion.7
  217.6 3.3 fusion.1
  221.0 2.7 copy.21
  223.6 2.5 fusion.9
  226.1 188.9 %custom-call.31 = f32[64,32,32]{2,1,0:T(8,128)} custom-call(f32[64,32,32]{2,1,0:T(8,128)} %fusion.9), custom_call_target="Cholesky" | custom-call | tf_op jit(solution)/shard_map/jit(cholesky)/cholesky | solution.py:59
  415.0 1.8 copy.22
  417.2 13.4 %custom-call.32 = f32[64,1,32,32]{0,2,3,1:T(8,128)} custom-call(f32[64,1,32,32]{0,3,2,1:T(8,128)S(1)} %select_bitcast_fusion), custom_call_target="InvertDiagBlocksLowerTriangular" | custom-call | tf_op jit(solution)/shard_map/jit(_solve_triangular)/vmap()/triangular_solve | solution.py:61
  430.6 2.0 copy.35
  432.6 1.0 convolution_bitcast_fusion.1
  433.6 1.7 convolution_bitcast_fusion
  435.4 1.1 fusion.48
  (69 shorter events, 8.3 us)
Async XLA Ops:
  6.5 30.1 %copy-start = (s32[8192]{0:T(1024)S(1)}, s32[8192]{0:T(1024)}, u32[]{:S(2)}) copy-start(s32[8192]{0:T(1024)} %param.9) | copy-start | bytes 98308
  6.5 25.4 %all-gather.5.cloned.1.call-start = ((), (), s32[]{:S(2)}) async-start(), calls=%async_computation.1 | async-start | bytes 2621440 | tf_op jit(solution)/shard_map/all_gather | solution.py:15
  7.3 29.2 %copy-start.7 = (s32[64,32]{0,1:T(8,128)S(1)}, s32[64,32]{0,1:T(8,128)}, u32[]{:S(2)}) copy-start(s32[64,32]{0,1:T(8,128)} %param.7) | copy-start | bytes 24580
  7.3 107.1 %all-reduce.3.cloned.1.call-start = ((), (), s32[]{:S(2)}) async-start(), calls=%async_computation.2 | async-start | bytes 2097152 | tf_op jit(solution)/shard_map/psum | solution.py:19
  35.7 154.1 %all-gather.3.cloned.1.call-start = ((), (), s32[]{:S(2)}) async-start(), calls=%async_computation | async-start | bytes 4718592 | tf_op jit(solution)/shard_map/all_gather | solution.py:27
  36.7 12.1 %copy-start.4 = (bf16[64,256]{1,0:T(8,128)(2,1)S(1)}, bf16[64,256]{1,0:T(8,128)(2,1)}, u32[]{:S(2)}) copy-start(bf16[64,256]{1,0:T(8,128)(2,1)} %param.5) | copy-start | bytes 98308
  36.7 18.1 %copy-start.8 = (s32[64]{0:T(128)S(1)}, s32[64]{0:T(128)}, u32[]{:S(2)}) copy-start(s32[64]{0:T(128)} %param.8) | copy-start | bytes 772
  211.8 2.0 copy-start.2
  211.9 2.0 copy-start.3
  214.6 0.6 copy-start.5
  221.0 2.7 copy-start.1
  432.6 3.9 copy-start.6
Sparse Core Ops, SparseCore 0:
  8.9 23.0 all-gather.4
  35.8 78.4 all-reduce.2
  116.7 73.1 all-gather.2
where the time goes:
time: 446 us; the launch traced here: 444 us
  other arithmetic  262 us (59%)
  waiting for transfers between devices  97.3 us (22%)
  local copies, waits for them, and re-layouts  32.9 us (7%)
  matrix products  20.4 us (5%)
  blocking collectives  16.3 us (4%)
  between operations  14.8 us (3%)
    another operation x4, other arithmetic, on_device(): inner_factor = jnp.linalg.cholesky(inner)  189 us
    psum x1, waiting for transfers between devices, on_device(): gram_rows = lax.psum(gram_part, 'rows')  59.5 us
    another operation x6, other arithmetic, on_device(): shift_factor = jnp.linalg.cholesky(diag_shift)  34 us
    all_gather x1, waiting for transfers between devices, on_device(): lax.all_gather(item_table, 'dim', axis=1, tiled=True)  24.7 us
    another operation x3, other arithmetic, on_device(): jax.scipy.linalg.cho_solve((shift_factor, True), jnp.eye(width, dtype=jnp...  19.7 us
    another operation x3, other arithmetic, on_device(): jax.scipy.linalg.solve_triangular(inner_factor, middle, lower=True, trans...  13.6 us
    gather x1, local copies, waits for them, and re-layouts, on_device(): table_rows = item_row[observed_items]  11.8 us
    all_gather x1, waiting for transfers between devices, on_device(): shard_rows = lax.all_gather(item_table, 'rows', axis=0, tiled=True)  11.7 us
  transfers between devices with their start and end apart: 3, of which 3 were waited for; matrix products, arithmetic and copies ran while one was open for 17% of the time, Pallas kernels for 0%

commit v1 on v0

v1 whole, which is shorter than its diff:
```python
import functools

import jax
import jax.numpy as jnp
from jax import lax
from jax.experimental import pallas as pl
from jax.experimental.pallas import tpu as pltpu
from jax.sharding import PartitionSpec as P

F32 = jnp.float32
BF16 = jnp.bfloat16
HIGHEST = lax.Precision.HIGHEST
PANEL = 32


def split3(x):
    high = x.astype(BF16)
    rest = x - high.astype(F32)
    middle = rest.astype(BF16)
    low = (rest - middle.astype(F32)).astype(BF16)
    return high, middle, low


def dot(a, b, dims):
    return lax.dot_general(a, b, (dims, ((), ())), preferred_element_type=F32)


def exact_dot(a, b, dims):
    return lax.dot_general(
        a, b, (dims, ((), ())), precision=HIGHEST, preferred_element_type=F32
    )


def inverse_kernel(weight, gram_ref, out_ref, work):
    width = gram_ref.shape[0]
    rows = lax.broadcasted_iota(jnp.int32, (width, width), 0)
    columns = lax.broadcasted_iota(jnp.int32, (width, width), 1)
    work[...] = weight * gram_ref[...] + jnp.where(rows == columns, 1.0, 0.0)
    panel_rows = lax.broadcasted_iota(jnp.int32, (PANEL, 1), 0)
    panel_columns = lax.broadcasted_iota(jnp.int32, (PANEL, width), 1)
    for panel in range(width // PANEL):
        first = panel * PANEL
        mine = (panel_columns >= first) & (panel_columns < first + PANEL)
        before = work[first:first + PANEL, :]
        after = before
        for step in range(PANEL):
            column = after[:, first + step:first + step + 1]
            inverse = 1.0 / column[step:step + 1, :]
            unit = jnp.where(panel_rows == step, 1.0, 0.0)
            after = jnp.where(panel_columns == first + step, unit, after)
            scaled = after[step:step + 1, :] * inverse
            after = jnp.where(panel_rows == step, scaled, after - column * scaled)
        after = jnp.where(mine, -after, after)
        sign = jnp.where(panel_columns == first + lax.broadcasted_iota(jnp.int32, (PANEL, width), 0), -1.0, 0.0)
        before = jnp.where(mine, sign, before)
        b1, b2, b3 = split3(before)
        a1, a2, a3 = split3(after)
        left = jnp.concatenate([b1, b1, b2, b1, b2, b3], axis=0)
        right = jnp.concatenate([a1, a2, a1, a3, a2, a1], axis=0)
        change = dot(left, right, ((0,), (0,)))
        outside = ((rows < first) | (rows >= first + PANEL)) & (
            (columns < first) | (columns >= first + PANEL)
        )
        work[...] = jnp.where(outside, work[...], 0.0) - change
    out_ref[...] = -work[...]


def own_slots(users, list_len):
    row = lax.broadcasted_iota(jnp.int32, (users, users * list_len), 0)
    column = lax.broadcasted_iota(jnp.int32, (users, users * list_len), 1)
    return (column >= row * list_len) & (column < (row + 1) * list_len)


def fold_lanes(x, list_len):
    lanes = 128
    total = x[:, :lanes]
    for part in range(1, x.shape[1] // lanes):
        total = total + x[:, part * lanes:(part + 1) * lanes]
    result = total[:, :list_len]
    for part in range(1, lanes // list_len):
        result = result + total[:, part * list_len:(part + 1) * list_len]
    return result


def spread_lanes(x, users):
    lanes = 128
    tile = jnp.concatenate([x] * (lanes // x.shape[1]), axis=1)
    return jnp.concatenate([tile] * (users * x.shape[1] // lanes), axis=1)


def solve_kernel(
    weight, rows_ref, live_ref, predicted_ref, inverse_ref, times_ref, own_ref, out_ref,
    scaled, folded, system,
):
    users, list_len = live_ref.shape
    own = own_ref[...].astype(F32)
    h = rows_ref[...]
    mask = own_slots(users, list_len)
    residual = live_ref[...] * (predicted_ref[...] - 1.0)
    spread = jnp.where(mask, spread_lanes(residual, users), 0.0)
    gradient = weight * times_ref[...] + own
    for piece in split3(spread):
        gradient = gradient + dot(piece, h, ((1,), (0,)))
    inverse = inverse_ref[...]
    scaled_grad = exact_dot(gradient, inverse, ((1,), (0,)))
    projected = jnp.zeros((users, users * list_len), F32)
    for piece in split3(scaled_grad):
        projected = projected + dot(piece, h, ((1,), (1,)))
    projected = fold_lanes(jnp.where(mask, projected, 0.0), list_len).T

    inverse_pieces = split3(inverse)
    group = 8 * list_len
    block_row = lax.broadcasted_iota(jnp.int32, (group, group), 0) // list_len
    block_column = lax.broadcasted_iota(jnp.int32, (group, group), 1) // list_len
    for start in range(0, users * list_len, group):
        here = rows_ref[start:start + group, :]
        x = sum(dot(here, piece, ((1,), (0,))) for piece in inverse_pieces)
        inner = sum(dot(piece, here, ((1,), (1,))) for piece in split3(x))
        inner = jnp.where(block_row == block_column, inner, 0.0)
        folded[start:start + group, :] = fold_lanes(inner, list_len)
    slot = lax.broadcasted_iota(jnp.int32, (list_len, users), 0)
    head = lax.broadcasted_iota(jnp.int32, (8, users), 0)
    for i in range(list_len):
        block = folded[pl.ds(i, users, stride=list_len), :].T
        system[i, :list_len, :] = block + jnp.where(slot == i, 1.0, 0.0)
        system[i, list_len:, :] = jnp.where(head == 0, projected[i:i + 1, :], 0.0)
    for k in range(list_len):
        first = k // 8 * 8
        pivot_row = system[k, first:, :]
        pivot_row = pivot_row * (1.0 / system[k, k:k + 1, :])
        for i in range(list_len):
            if i != k:
                system[i, first:, :] = system[i, first:, :] - system[i, k:k + 1, :] * pivot_row
    weights = jnp.concatenate(
        [system[i, list_len:list_len + 1, :] / system[i, i:i + 1, :] for i in range(list_len)], axis=0
    ).T
    spread = jnp.where(mask, spread_lanes(weights, users), 0.0)
    for piece in split3(spread):
        gradient = gradient - dot(piece, h, ((1,), (0,)))
    out_ref[...] = own - exact_dot(gradient, inverse, ((1,), (0,)))


def on_device(user_rows, item_table, observed_items, counts, item_row):
    width = user_rows.shape[1]
    users_dev, list_len = observed_items.shape
    weight_unobs = 32.0 / item_row.shape[0]
    vmem = pl.BlockSpec(memory_space=pltpu.VMEM)

    shard_rows = lax.all_gather(item_table, "rows", axis=0, tiled=True)
    full_rows = lax.all_gather(item_table, "dim", axis=1, tiled=True)
    all_users = lax.all_gather(lax.all_gather(user_rows, "dim", axis=1, tiled=True), "rows", axis=0, tiled=True)
    scores = dot(all_users, full_rows, ((1,), (1,)))
    times_part = exact_dot(scores, item_table.astype(F32), ((1,), (0,)))
    gram_times = lax.psum_scatter(times_part, "rows", scatter_dimension=0, tiled=True)
    diag_gram = dot(shard_rows, shard_rows, ((0,), (0,)))

    table_rows = item_row[observed_items]
    live = lax.broadcasted_iota(jnp.int32, (users_dev, list_len), 1) < counts[:, None]
    picked = shard_rows[table_rows]
    fetched = jnp.where(live[..., None], picked, jnp.zeros_like(picked))
    predicted = lax.psum(
        jnp.einsum("ub,ujb->uj", user_rows, fetched, preferred_element_type=F32), "dim"
    )

    inverse = pl.pallas_call(
        functools.partial(inverse_kernel, weight_unobs),
        out_shape=jax.ShapeDtypeStruct((width, width), F32),
        in_specs=[vmem],
        out_specs=vmem,
        scratch_shapes=[pltpu.VMEM((width, width), F32)],
        name="inverse",
    )(diag_gram)
    return pl.pallas_call(
        functools.partial(solve_kernel, weight_unobs),
        out_shape=jax.ShapeDtypeStruct((users_dev, width), F32),
        in_specs=[vmem] * 6,
        out_specs=vmem,
        scratch_shapes=[
            pltpu.VMEM((8, 128), F32),
            pltpu.VMEM((users_dev * list_len, list_len), F32),
            pltpu.VMEM((list_len, list_len + 8, users_dev), F32),
        ],
        compiler_params=pltpu.CompilerParams(vmem_limit_bytes=48 * 1024 * 1024),
        name="solve",
    )(
        fetched.reshape(users_dev * list_len, width), live.astype(F32), predicted, inverse,
        gram_times, user_rows,
    )


def solution(mesh):
    in_specs = (P("rows", "dim"), P("rows", "dim"), P("rows", None), P("rows"), P())
    out_specs = P("rows", "dim")
    return jax.shard_map(
        on_device, mesh=mesh, in_specs=in_specs, out_specs=out_specs, check_vma=False
    )
```

time: 446 us -> 237 us (0.53)
  other arithmetic: 262 us -> 1.27 us
  waiting for transfers between devices: 97.3 us -> 135 us
  Pallas kernels: 0 us -> 34.9 us
  local copies, waits for them, and re-layouts: 32.9 us -> 22.4 us
  matrix products: 20.4 us -> 11 us
    another operation x16 -> x0, other arithmetic: 256 us -> none  [the longest x4 189 us: on_device(): inner_factor = jnp.linalg.cholesky(inner)]
    psum x1 -> x0, waiting for transfers between devices: 59.5 us -> none  [on_device(): gram_rows = lax.psum(gram_part, 'rows')]
    all_gather x1, waiting for transfers between devices: 11.7 us -> 70.7 us  [on_device(): shard_rows = lax.all_gather(item_table, 'rows', axis=0, tiled=True)]
    pallas_call x0 -> x2, Pallas kernels: none -> 34.9 us  [the longest x1 24.4 us: on_device(): pl.pallas_call(functools.partial(inverse_kernel, weight_unobs), out_shape...]
    all_gather x1 -> x2, waiting for transfers between devices: 24.7 us -> 49.2 us  [the longest x1 26 us: on_device(): lax.all_gather(lax.all_gather(user_rows, 'dim', axis=1, tiled=True), 'row...]
    reduce_scatter x0 -> x1, waiting for transfers between devices: none -> 13.5 us  [on_device(): lax.psum_scatter(times_part, 'rows', scatter_dimension=0, tiled=True)]
    another operation x11 -> x0, local copies, waits for them, and re-layouts: 7.87 us -> none
    another operation x10 -> x0, matrix products: 5.02 us -> none  [the longest x6 1.8 us: on_device(): jax.scipy.linalg.cho_solve((shift_factor, True), jnp.eye(width, dtype=jnp...]
  transfers between devices with their start and end apart: 3 -> 4, of which waited for: 3 -> 4; matrix products, arithmetic and copies ran while one was open for 17% -> 14% of each run, Pallas kernels for 0% -> 10%
where the time goes in v1:
time: 237 us; the launch traced here: 234 us
  waiting for transfers between devices  135 us (57%)
  Pallas kernels  34.9 us (15%)
  local copies, waits for them, and re-layouts  22.4 us (9%)
  blocking collectives  16.7 us (7%)
  between operations  13.2 us (6%)
  matrix products  11 us (5%)
    all_gather x1, waiting for transfers between devices, on_device(): shard_rows = lax.all_gather(item_table, 'rows', axis=0, tiled=True)  70.7 us
    all_gather x1, waiting for transfers between devices, on_device(): lax.all_gather(lax.all_gather(user_rows, 'dim', axis=1, tiled=True), 'row...  26 us
    pallas_call x1, Pallas kernels, on_device(): pl.pallas_call(functools.partial(inverse_kernel, weight_unobs), out_shape...  24.4 us
    all_gather x1, waiting for transfers between devices, on_device(): full_rows = lax.all_gather(item_table, 'dim', axis=1, tiled=True)  23.2 us
    reduce_scatter x1, waiting for transfers between devices, on_device(): lax.psum_scatter(times_part, 'rows', scatter_dimension=0, tiled=True)  13.5 us
    gather x2, local copies, waits for them, and re-layouts, on_device(): table_rows = item_row[observed_items]  11.9 us
    pallas_call x1, Pallas kernels, on_device(): pl.pallas_call(functools.partial(solve_kernel, weight_unobs), out_shape=j...  10.5 us
    psum x1, blocking collectives, on_device(): lax.psum(jnp.einsum('ub,ujb->uj', user_rows, fetched, preferred_element_t...  10.5 us
  transfers between devices with their start and end apart: 4, of which 4 were waited for; matrix products, arithmetic and copies ran while one was open for 14% of the time, Pallas kernels for 10%

profile of v1, /device:TPU:12, one launch (start us, length us, event | category | flops | bytes accessed | tf_op | source)
XLA Modules:
  0.0 234.5 jit_solution(4269589187713854329)
XLA Ops:
  6.5 6.2 %all_gather.13 = bf16[64,1024]{1,0:T(8,128)(2,1)} all-gather(bf16[64,256]{1,0:T(8,128)(2,1)} %own_ref.1), channel_id=1, replica_groups=mesh['dim'=4,'rows'=8] {'dim'}, dimensions={1}, use_global_device_ids=true | all-gather | bytes 163840 | tf_op jit(solution)/shard_map/all_gather | solution.py:151
  12.8 0.0 all-gather.6.cloned.1.call-update
  12.8 0.0 all-gather.8.cloned.1.call-start
  12.8 0.7 all-gather.8.cloned.1.call-update
  13.5 0.0 all-gather.4.cloned.1.call-start
  13.6 0.7 all-gather.4.cloned.1.call-update
  14.3 0.0 reduce-scatter.2.cloned.1.call-start
  14.3 0.7 compare_select_fusion.1
  15.1 0.1 copy.6
  15.1 0.1 reshape.40
  15.2 0.0 copy-start.5
  15.2 11.8 %gather_fusion = s32[2048]{0:T(1024)S(1)} fusion(s32[8192]{0:T(1024)S(1)} %copy-done, s32[2048]{0:T(1024)S(1)} %broadcast_clamp_fusion), kind=kCustom, calls=%fused_computation | custom fusion | bytes 24576 | tf_op jit(solution)/shard_map/gather | solution.py:157
  27.0 0.1 gather.11
  27.1 0.1 reshape.48
  27.2 0.1 fusion.6
  27.3 0.1 lt.31
  27.4 0.0 copy-start.4
  27.4 26.0 %all-gather.6.cloned.1.call-done = bf16[512,1024]{1,0:T(8,128)(2,1)} async-done(((bf16[64,1024]{1,0:T(8,128)(2,1)}), bf16[512,1024]{1,0:T(8,128)(2,1)}) %all-gather.6.cloned.1.call-update) | async-done | bytes 1048592 | tf_op jit(solution)/shard_map/all_gather | solution.py:151
  53.3 23.2 %all-gather.8.cloned.1.call-done = bf16[1024,1024]{1,0:T(8,128)(2,1)} async-done(((bf16[1024,256]{1,0:T(8,128)(2,1)}), bf16[1024,1024]{1,0:T(8,128)(2,1)}) %all-gather.8.cloned.1.call-update) | async-done | bytes 2097168 | tf_op jit(solution)/shard_map/all_gather | solution.py:150
  76.6 3.2 %fusion.8 = f32[512,1024]{1,0:T(8,128)S(1)} fusion(bf16[512,1024]{1,0:T(8,128)(2,1)} %all-gather.6.cloned.1.call-done, bf16[1024,1024]{1,0:T(8,128)(2,1)} %all-gather.8.cloned.1.call-done), kind=kOutput, calls=%fused_computation.16 | convolution fusion | flops 1073741824 | bytes 5242880 | tf_op jit(solution)/shard_map/dot_general | solution.py:25
  79.8 1.9 fusion.9
  81.7 0.0 reduce-scatter.2.cloned.1.call-update
  81.7 70.7 %all-gather.4.cloned.1.call-done = bf16[8192,256]{1,0:T(8,128)(2,1)} async-done(((bf16[1024,256]{1,0:T(8,128)(2,1)}), bf16[8192,256]{1,0:T(8,128)(2,1)}) %all-gather.4.cloned.1.call-update) | async-done | bytes 4194320 | tf_op jit(solution)/shard_map/all_gather | solution.py:149
  152.4 5.4 %fusion.7.gram_ref = f32[256,256]{1,0:T(8,128)} fusion(bf16[8192,256]{1,0:T(8,128)(2,1)} %all-gather.4.cloned.1.call-done), kind=kOutput, calls=%fused_computation.15 | convolution fusion | flops 1073741824 | bytes 4456448 | tf_op jit(solution)/shard_map/dot_general | solution.py:25
  157.8 24.4 %inverse.1.inverse_ref = f32[256,256]{1,0:T(8,128)} custom-call(f32[256,256]{1,0:T(8,128)} %fusion.7.gram_ref), custom_call_target="tpu_custom_call" | custom-call | tf_op jit(solution)/shard_map/inverse/pallas_call | solution.py:165
  182.2 9.4 %gather_fusion.1 = bf16[2048,256]{1,0:T(8,128)(2,1)S(1)} fusion(bf16[8192,256]{1,0:T(8,128)(2,1)} %all-gather.4.cloned.1.call-done, s32[2048]{0:T(1024)S(1)} %broadcast_clamp_fusion.1), kind=kCustom, calls=%fused_computation.1 | custom fusion | bytes 2105344 | tf_op jit(solution)/shard_map/gather | solution.py:159
  191.7 0.4 fusion
  192.1 10.5 %psum.7.predicted_ref = f32[64,32]{1,0:T(8,128)S(1)} all-reduce(f32[64,32]{1,0:T(8,128)S(1)} %bitcast.14), channel_id=1, replica_groups=mesh['dim'=4,'rows'=8] {'dim'}, use_global_device_ids=true, to_apply=%region_0.0 | all-reduce | flops 2048 | bytes 16384 | tf_op jit(solution)/shard_map/psum | solution.py:161
  202.6 0.4 broadcast_select_fusion.rows_ref
  203.0 13.5 %reduce-scatter.2.cloned.1.call-done.times_ref = f32[64,256]{1,0:T(8,128)} async-done(((f32[512,256]{1,0:T(8,128)}), f32[64,256]{1,0:T(8,128)}) %reduce-scatter.2.cloned.1.call-update) | async-done | bytes 65552 | tf_op jit(solution)/shard_map/reduce_scatter | solution.py:154
  216.5 0.8 copy-done.3
  217.4 10.5 %solve.1 = f32[64,256]{1,0:T(8,128)} custom-call(bf16[2048,256]{1,0:T(8,128)(2,1)S(1)} %broadcast_select_fusion.rows_ref, f32[64,32]{1,0:T(8,128)S(1)} %get-tuple-element.5.live_ref, f32[64,32]{1,0:T(8,128)S(1)} %psum.7.predicted_ref, f32[256,256]{1,0:T(8,128)S(1)} %copy-done.1, f32[64,256]{1,0:T(8,128)S(1)} %copy-done.3, bf16[64,256]{1,0:T(8,128)(2,1)S(1)} %copy-done.2), custom_call_target="tpu_custom_call" | custom-call | tf_op jit(solution)/shard_map/solve/pallas_call | solution.py:173
  (13 shorter events, 0.0 us)
Async XLA Ops:
  6.5 8.7 %copy-start = (s32[8192]{0:T(1024)S(1)}, s32[8192]{0:T(1024)}, u32[]{:S(2)}) copy-start(s32[8192]{0:T(1024)} %param.9) | copy-start | bytes 98308
  6.5 46.8 %all-gather.6.cloned.1.call-start = ((), (), s32[]{:S(2)}) async-start(), calls=%async_computation.2 | async-start | bytes 1179648 | tf_op jit(solution)/shard_map/all_gather | solution.py:151
  12.8 63.8 %all-gather.8.cloned.1.call-start = ((), (), s32[]{:S(2)}) async-start(), calls=%async_computation.3 | async-start | bytes 2621440 | tf_op jit(solution)/shard_map/all_gather | solution.py:150
  13.5 138.8 %all-gather.4.cloned.1.call-start = ((), (), s32[]{:S(2)}) async-start(), calls=%async_computation.1 | async-start | bytes 4718592 | tf_op jit(solution)/shard_map/all_gather | solution.py:149
  14.3 202.2 %reduce-scatter.2.cloned.1.call-start = ((), (), s32[]{:S(2)}) async-start(), calls=%async_computation.4 | async-start | bytes 589824 | tf_op jit(solution)/shard_map/reduce_scatter | solution.py:154
  15.2 12.0 %copy-start.5 = (s32[64]{0:T(128)S(1)}, s32[64]{0:T(128)}, u32[]{:S(2)}) copy-start(s32[64]{0:T(128)} %param.8) | copy-start | bytes 772
  27.4 52.4 %copy-start.4 = (bf16[1024,256]{1,0:T(8,128)(2,1)S(1)}, bf16[1024,256]{1,0:T(8,128)(2,1)}, u32[]{:S(2)}) copy-start(bf16[1024,256]{1,0:T(8,128)(2,1)} %param.6) | copy-start | bytes 1572868
  182.2 9.4 %copy-start.2 = (bf16[64,256]{1,0:T(8,128)(2,1)S(1)}, bf16[64,256]{1,0:T(8,128)(2,1)}, u32[]{:S(2)}) copy-start(bf16[64,256]{1,0:T(8,128)(2,1)} %own_ref.1) | copy-start | bytes 98308
  191.7 24.9 %copy-start.1 = (f32[256,256]{1,0:T(8,128)S(1)}, f32[256,256]{1,0:T(8,128)}, u32[]{:S(2)}) copy-start(f32[256,256]{1,0:T(8,128)} %inverse.1.inverse_ref) | copy-start | bytes 786436
  216.5 0.8 copy-start.3
Sparse Core Ops, SparseCore 0:
  12.9 40.3 all-gather.5
  54.9 21.6 all-gather.7
  78.7 73.6 all-gather.3
  155.6 60.8 reduce-scatter.1

commit v2 on v1

--- a/solution.py
+++ b/solution.py
@@ -140,21 +140,247 @@
     out_ref[...] = own - exact_dot(gradient, inverse, ((1,), (0,)))
 
 
+MESH = pl.DeviceIdType.MESH
+
+
+def ring_place(index, n):
+    odd = lax.rem(index, 2)
+    return (1 - odd) * lax.div(index, 2) + odd * (n // 2 + lax.div(n - 1 - index, 2))
+
+
+def ring_index(place, n):
+    high = lax.div(place, n // 2)
+    return (1 - high) * 2 * place + high * (n - 1 - 2 * (place - n // 2))
+
+
+def exchange_kernel(
+    n_rows, n_dim, table_ref, users_ref, gathered_ref, gram_ref, times_ref,
+    held, tables, users, staged, arrived,
+    ring_send, ring_recv, out_sem, first_send, first_recv, table_send, table_recv,
+    users_send, users_recv, sum_send, sum_recv,
+):
+    me_row = lax.axis_index("rows")
+    me_dim = lax.axis_index("dim")
+    items, width = table_ref.shape
+    users_dev = users_ref.shape[0]
+    half = n_rows // 2
+    levels = n_dim // 2
+    core = lax.rem(me_dim, 2)
+    partner = me_dim + 1 - 2 * core
+    place = ring_place(me_row, n_rows)
+    right = ring_index(lax.rem(place + 1, n_rows), n_rows)
+    left = ring_index(lax.rem(place + n_rows - 1, n_rows), n_rows)
+
+    def row_peer(k):
+        return lax.rem(me_row + k, n_rows)
+
+    def dim_peer(k):
+        return lax.rem(me_dim + 2 * k, n_dim)
+
+    def dim_source(k):
+        return lax.rem(me_dim + n_dim - 2 * k, n_dim)
+
+    barrier = pltpu.get_barrier_semaphore()
+    for k in range(1, n_rows):
+        pl.semaphore_signal(barrier, inc=1, device_id={"rows": row_peer(k)}, device_id_type=MESH)
+    for k in range(1, levels):
+        pl.semaphore_signal(barrier, inc=1, device_id={"dim": dim_peer(k)}, device_id_type=MESH)
+    pl.semaphore_signal(barrier, inc=1, device_id={"dim": partner}, device_id_type=MESH)
+    pl.semaphore_wait(barrier, n_rows - 1 + levels)
+
+    def remote(src, dst, send, recv, device):
+        copy = pltpu.make_async_remote_copy(
+            src_ref=src, dst_ref=dst, send_sem=send, recv_sem=recv,
+            device_id=device, device_id_type=MESH,
+        )
+        copy.start()
+        return copy
+
+    def block_of(index, start, size):
+        return held.at[pl.ds(index * items + start, size)]
+
+    def ring_step(step):
+        copies = []
+        last = step == half - 1
+        for way, to in ((0, right), (1, left)):
+            shift = n_rows - step if way == 0 else step
+            owner = ring_index(lax.rem(place + shift, n_rows), n_rows)
+            size = items // 2 if last else items
+            start = items // 2 if last and way == 1 else 0
+            target = block_of(owner, start, size)
+            copies.append(remote(
+                table_ref.at[pl.ds(start, size)] if step == 0 else target,
+                target, ring_send.at[way, step], ring_recv.at[way, step], {"rows": to},
+            ))
+        return copies
+
+    outs = []
+
+    def keep(index, start, size):
+        copy = pltpu.make_async_copy(
+            block_of(index, start, size),
+            gathered_ref.at[pl.ds(index * items + start, size)],
+            out_sem.at[len(outs)],
+        )
+        copy.start()
+        outs.append(copy)
+
+    def add_gram(index, start, size):
+        block = held[pl.ds(index * items + start, size), :]
+        gram_ref[...] += dot(block, block, ((0,), (0,)))
+
+    def ring_arrivals(step):
+        last = step == half - 1
+        found = []
+        for way in (0, 1):
+            shift = n_rows - step - 1 if way == 0 else step + 1
+            owner = ring_index(lax.rem(place + shift, n_rows), n_rows)
+            size = items // 2 if last else items
+            start = items // 2 if last and way == 1 else 0
+            found.append((owner, start, size))
+        return found
+
+    mine_users = pl.ds(me_row * users_dev, users_dev)
+    first = [
+        remote(users_ref, users.at[me_dim, mine_users], first_send.at[k], first_recv.at[k], {"rows": row_peer(k)})
+        for k in range(1, n_rows)
+    ]
+    ring = [ring_step(0)]
+    table_far = [
+        remote(table_ref, tables.at[me_dim], table_send.at[k], table_recv.at[k], {"dim": dim_peer(k)})
+        for k in range(1, levels)
+    ]
+    table_near = [remote(table_ref, tables.at[me_dim], table_send.at[0], table_recv.at[0], {"dim": partner})]
+    held[pl.ds(me_row * items, items), :] = table_ref[...]
+    tables[me_dim] = table_ref[...]
+    users[me_dim, mine_users, :] = users_ref[...]
+    gram_ref[...] = jnp.zeros_like(gram_ref)
+    keep(me_row, 0, items)
+    add_gram(me_row, 0, items)
+
+    for copy in first:
+        copy.wait_recv()
+    users_far = [
+        remote(users.at[me_dim], users.at[me_dim], users_send.at[k], users_recv.at[k], {"dim": dim_peer(k)})
+        for k in range(1, levels)
+    ]
+    users_near = [remote(users.at[me_dim], users.at[me_dim], users_send.at[0], users_recv.at[0], {"dim": partner})]
+    sums = []
+
+    def relay():
+        for k in range(1, levels):
+            source = dim_source(k)
+            table_far[k - 1].wait_recv()
+            table_near.append(remote(
+                tables.at[source], tables.at[source], table_send.at[levels + k], table_recv.at[levels + k], {"dim": partner},
+            ))
+            users_far[k - 1].wait_recv()
+            users_near.append(remote(
+                users.at[source], users.at[source], users_send.at[levels + k], users_recv.at[levels + k], {"dim": partner},
+            ))
+
+    def score():
+        for copy in table_near + users_near:
+            copy.wait_recv()
+        total = n_rows * users_dev
+        chunk = min(256, total)
+        pieces_of_table = table_ref[...]
+        for start in range(0, total, chunk):
+            scores = dot(users[0, start:start + chunk, :], tables[0], ((1,), (1,)))
+            for d in range(1, n_dim):
+                scores = scores + dot(users[d, start:start + chunk, :], tables[d], ((1,), (1,)))
+            part = sum(dot(piece, pieces_of_table, ((1,), (0,))) for piece in split3(scores))
+            staged[start:start + chunk, :] = part
+        for k in range(1, n_rows):
+            sums.append(remote(
+                staged.at[pl.ds(row_peer(k) * users_dev, users_dev)], arrived.at[k],
+                sum_send.at[k], sum_recv.at[k], {"rows": row_peer(k)},
+            ))
+
+    for step in range(half):
+        for copy in ring[step]:
+            copy.wait_recv()
+        if step < half - 1:
+            ring.append(ring_step(step + 1))
+        for found in ring_arrivals(step):
+            keep(*found)
+            add_gram(*found)
+        if step == 0:
+            relay()
+        if step == 1:
+            score()
+
+    times = staged[mine_users, :]
+    for k in range(1, n_rows):
+        sums[k - 1].wait_recv()
+        times = times + arrived[k]
+    times_ref[...] = times
+    for copy in first + table_far + table_near + users_far + users_near + sums + ring[0]:
+        copy.wait_send()
+    for copies in ring[1:]:
+        for copy in copies:
+            copy.wait_send()
+    for copy in outs:
+        copy.wait()
+
+
+def exchange(item_table, user_rows, n_rows, n_dim):
+    items, width = item_table.shape
+    users_dev = user_rows.shape[0]
+    vmem = pl.BlockSpec(memory_space=pltpu.VMEM)
+    dma = pltpu.SemaphoreType.DMA
+    half = n_rows // 2
+    return pl.pallas_call(
+        functools.partial(exchange_kernel, n_rows, n_dim),
+        out_shape=[
+            jax.ShapeDtypeStruct((n_rows * items, width), BF16),
+            jax.ShapeDtypeStruct((width, width), F32),
+            jax.ShapeDtypeStruct((users_dev, width), F32),
+        ],
+        in_specs=[vmem] * 2,
+        out_specs=[pl.BlockSpec(memory_space=pl.ANY), vmem, vmem],
+        scratch_shapes=[
+            pltpu.VMEM((n_rows * items, width), BF16),
+            pltpu.VMEM((n_dim, items, width), BF16),
+            pltpu.VMEM((n_dim, n_rows * users_dev, width), BF16),
+            pltpu.VMEM((n_rows * users_dev, width), F32),
+            pltpu.VMEM((n_rows, users_dev, width), F32),
+            dma((2, half)),
+            dma((2, half)),
+            dma((n_rows + 1,)),
+            dma((n_rows,)),
+            dma((n_rows,)),
+            dma((n_dim,)),
+            dma((n_dim,)),
+            dma((n_dim,)),
+            dma((n_dim,)),
+            dma((n_rows,)),
+            dma((n_rows,)),
+        ],
+        compiler_params=pltpu.CompilerParams(
+            collective_id=0, has_side_effects=True, vmem_limit_bytes=56 * 1024 * 1024
+        ),
+        name="exchange",
+    )(item_table, user_rows)
+
+
 def on_device(user_rows, item_table, observed_items, counts, item_row):
     width = user_rows.shape[1]
     users_dev, list_len = observed_items.shape
     weight_unobs = 32.0 / item_row.shape[0]
     vmem = pl.BlockSpec(memory_space=pltpu.VMEM)
 
-    shard_rows = lax.all_gather(item_table, "rows", axis=0, tiled=True)
-    full_rows = lax.all_gather(item_table, "dim", axis=1, tiled=True)
-    all_users = lax.all_gather(lax.all_gather(user_rows, "dim", axis=1, tiled=True), "rows", axis=0, tiled=True)
-    scores = dot(all_users, full_rows, ((1,), (1,)))
-    times_part = exact_dot(scores, item_table.astype(F32), ((1,), (0,)))
-    gram_times = lax.psum_scatter(times_part, "rows", scatter_dimension=0, tiled=True)
-    diag_gram = dot(shard_rows, shard_rows, ((0,), (0,)))
-
-    table_rows = item_row[observed_items]
+    shard_rows, diag_gram, gram_times = exchange(
+        item_table, user_rows, lax.axis_size("rows"), lax.axis_size("dim")
+    )
+
+    slots = observed_items.reshape(-1, 1)
+    lines = item_row.reshape(-1, 128).astype(F32)
+    line_of = lax.broadcasted_iota(jnp.int32, (1, lines.shape[0]), 1) == slots // 128
+    chosen = exact_dot(line_of.astype(F32), lines, ((1,), (0,)))
+    lane_of = lax.broadcasted_iota(jnp.int32, (1, 128), 1) == slots % 128
+    table_rows = jnp.sum(jnp.where(lane_of, chosen, 0.0), axis=1).astype(jnp.int32)
+    table_rows = table_rows.reshape(observed_items.shape)
     live = lax.broadcasted_iota(jnp.int32, (users_dev, list_len), 1) < counts[:, None]
     picked = shard_rows[table_rows]
     fetched = jnp.where(live[..., None], picked, jnp.zeros_like(picked))

time: 237 us -> 127 us (0.54); the launches traced: 234 us -> 127 us
  waiting for transfers between devices: 135 us -> 0 us
  Pallas kernels: 34.9 us -> 102 us
  between operations: 13.2 us -> 0.11 us
  local copies, waits for them, and re-layouts: 22.4 us -> 11.5 us
  matrix products: 11 us -> 2.42 us
  blocking collectives: 16.7 us -> 10.5 us
    all_gather x3 -> x0, waiting for transfers between devices: 120 us -> none  [the longest x1 70.7 us: on_device(): shard_rows = lax.all_gather(item_table, 'rows', axis=0, tiled=True)]
    pallas_call x0 -> x1, Pallas kernels: none -> 67.1 us  [exchange(): pl.pallas_call(functools.partial(exchange_kernel, n_rows, n_dim), out_sha...]
    reduce_scatter x1 -> x0, waiting for transfers between devices: 13.5 us -> none  [on_device(): lax.psum_scatter(times_part, 'rows', scatter_dimension=0, tiled=True)]
    gather x2 -> x0, local copies, waits for them, and re-layouts: 11.9 us -> none  [on_device(): table_rows = item_row[observed_items]]
    dot_general x2 -> x0, matrix products: 8.65 us -> none  [dot(): return lax.dot_general(a, b, (dims, ((), ())), preferred_element_type=F32)]
    all_gather x1 -> x0, blocking collectives: 6.23 us -> none  [on_device(): lax.all_gather(user_rows, 'dim', axis=1, tiled=True)]
  transfers between devices with their start and end apart: 4 -> 0, of which waited for: 4 -> 0; matrix products, arithmetic and copies ran while one was open for 14% -> 0% of each run, Pallas kernels for 10% -> 0%
where the time goes in v2:
time: 127 us
  Pallas kernels  102 us (80%)
  local copies, waits for them, and re-layouts  11.5 us (9%)
  blocking collectives  10.5 us (8%)
  matrix products  2.42 us (2%)
    pallas_call x1, Pallas kernels, exchange(): pl.pallas_call(functools.partial(exchange_kernel, n_rows, n_dim), out_sha...  67.1 us
    pallas_call x1, Pallas kernels, on_device(): pl.pallas_call(functools.partial(inverse_kernel, weight_unobs), out_shape...  24.4 us
    psum x1, blocking collectives, on_device(): lax.psum(jnp.einsum('ub,ujb->uj', user_rows, fetched, preferred_element_t...  10.5 us
    pallas_call x1, Pallas kernels, on_device(): pl.pallas_call(functools.partial(solve_kernel, weight_unobs), out_shape=j...  10.5 us
    gather x1, local copies, waits for them, and re-layouts, on_device(): picked = shard_rows[table_rows]  9.38 us

profile of v2, /device:TPU:12, one launch (start us, length us, event | category | flops | bytes accessed | tf_op | source)
XLA Modules:
  0.0 127.0 jit_solution(14634466815757141670)
XLA Ops:
  0.0 67.1 %exchange.1 = (bf16[8192,256]{1,0:T(8,128)(2,1)}, f32[256,256]{1,0:T(8,128)}, f32[64,256]{1,0:T(8,128)}) custom-call(bf16[1024,256]{1,0:T(8,128)(2,1)} %table_ref.1, bf16[64,256]{1,0:T(8,128)(2,1)} %own_ref.1), custom_call_target="tpu_custom_call" | custom-call | tf_op jit(solution)/shard_map/exchange/pallas_call | solution.py:333
  67.1 0.8 copy.6
  67.9 0.1 reshape.139
  68.0 2.0 %fusion = f32[2048]{0:T(1024)S(1)} fusion(s32[2048]{0:T(1024)S(1)} %get-tuple-element.12, s32[2048]{0:T(1024)S(1)} %get-tuple-element.11, s32[8192]{0:T(1024)} %param.9), kind=kOutput, calls=%fused_computation.2 | convolution fusion | flops 202250240 | bytes 57344 | tf_op jit(solution)/shard_map/dot_general | solution.py:29
  70.0 0.1 convert_element_type.27
  70.1 0.1 reshape.142
  70.2 0.0 copy-start.3
  70.2 0.0 copy-start.1
  70.2 9.4 %gather_fusion = bf16[2048,256]{1,0:T(8,128)(2,1)S(1)} fusion(bf16[8192,256]{1,0:T(8,128)(2,1)} %get-tuple-element.8, s32[2048]{0:T(1024)S(1)} %broadcast_clamp_fusion), kind=kCustom, calls=%fused_computation | custom fusion | bytes 2105344 | tf_op jit(solution)/shard_map/gather | solution.py:385
  79.6 0.0 copy-done.3
  79.6 0.0 copy-start.2
  79.6 0.1 fusion.12
  79.7 0.1 lt.37
  79.8 0.4 broadcast_select_fusion.rows_ref
  80.2 0.0 copy-done.1
  80.2 0.4 fusion.1
  80.7 10.5 %psum.7.predicted_ref = f32[64,32]{1,0:T(8,128)S(1)} all-reduce(f32[64,32]{1,0:T(8,128)S(1)} %bitcast.11), channel_id=1, replica_groups=mesh['dim'=4,'rows'=8] {'dim'}, use_global_device_ids=true, to_apply=%region_1.2 | all-reduce | flops 2048 | bytes 16384 | tf_op jit(solution)/shard_map/psum | solution.py:387
  91.2 24.4 %inverse.1.inverse_ref = f32[256,256]{1,0:T(8,128)} custom-call(f32[256,256]{1,0:T(8,128)} %get-tuple-element.9.gram_ref), custom_call_target="tpu_custom_call" | custom-call | tf_op jit(solution)/shard_map/inverse/pallas_call | solution.py:391
  115.6 0.0 copy-done.2
  115.6 0.0 copy-start
  115.6 0.9 copy-done
  116.5 10.5 %solve.1 = f32[64,256]{1,0:T(8,128)} custom-call(bf16[2048,256]{1,0:T(8,128)(2,1)S(1)} %broadcast_select_fusion.rows_ref, f32[64,32]{1,0:T(8,128)S(1)} %get-tuple-element.13.live_ref, f32[64,32]{1,0:T(8,128)S(1)} %psum.7.predicted_ref, f32[256,256]{1,0:T(8,128)S(1)} %copy-done, f32[64,256]{1,0:T(8,128)S(1)} %copy-done.2, bf16[64,256]{1,0:T(8,128)(2,1)S(1)} %copy-done.1), custom_call_target="tpu_custom_call" | custom-call | tf_op jit(solution)/shard_map/solve/pallas_call | solution.py:399
  (4 shorter events, 0.0 us)
Async XLA Ops:
  70.2 9.4 %copy-start.3 = (s32[64]{0:T(128)S(1)}, s32[64]{0:T(128)}, u32[]{:S(2)}) copy-start(s32[64]{0:T(128)} %param.8) | copy-start | bytes 772
  70.2 10.0 %copy-start.1 = (bf16[64,256]{1,0:T(8,128)(2,1)S(1)}, bf16[64,256]{1,0:T(8,128)(2,1)}, u32[]{:S(2)}) copy-start(bf16[64,256]{1,0:T(8,128)(2,1)} %own_ref.1) | copy-start | bytes 98308
  79.6 36.0 %copy-start.2 = (f32[64,256]{1,0:T(8,128)S(1)}, f32[64,256]{1,0:T(8,128)}, u32[]{:S(2)}) copy-start(f32[64,256]{1,0:T(8,128)} %get-tuple-element.10.times_ref) | copy-start | bytes 196612
  115.6 1.0 copy-start

commit v3 on v2

--- a/solution.py
+++ b/solution.py
@@ -11,6 +11,7 @@
 BF16 = jnp.bfloat16
 HIGHEST = lax.Precision.HIGHEST
 PANEL = 32
+GROUP = 8
 
 
 def split3(x):
@@ -43,13 +44,24 @@
         mine = (panel_columns >= first) & (panel_columns < first + PANEL)
         before = work[first:first + PANEL, :]
         after = before
-        for step in range(PANEL):
-            column = after[:, first + step:first + step + 1]
-            inverse = 1.0 / column[step:step + 1, :]
-            unit = jnp.where(panel_rows == step, 1.0, 0.0)
-            after = jnp.where(panel_columns == first + step, unit, after)
-            scaled = after[step:step + 1, :] * inverse
-            after = jnp.where(panel_rows == step, scaled, after - column * scaled)
+        for group in range(0, PANEL, GROUP):
+            spread = [
+                jnp.broadcast_to(after[:, c:c + 1], (PANEL, 128))
+                for c in range(first + group, first + group + GROUP)
+            ]
+            for step in range(group, group + GROUP):
+                column = spread[step - group]
+                inverse = 1.0 / column[step:step + 1, :]
+                for later in range(step - group + 1, GROUP):
+                    other = spread[later]
+                    scaled = other[step:step + 1, :] * inverse
+                    spread[later] = jnp.where(panel_rows == step, scaled, other - column * scaled)
+                wide = jnp.concatenate([column] * (width // 128), axis=1)
+                wide_inverse = jnp.concatenate([inverse] * (width // 128), axis=1)
+                unit = jnp.where(panel_rows == step, 1.0, 0.0)
+                after = jnp.where(panel_columns == first + step, unit, after)
+                scaled = after[step:step + 1, :] * wide_inverse
+                after = jnp.where(panel_rows == step, scaled, after - wide * scaled)
         after = jnp.where(mine, -after, after)
         sign = jnp.where(panel_columns == first + lax.broadcasted_iota(jnp.int32, (PANEL, width), 0), -1.0, 0.0)
         before = jnp.where(mine, sign, before)
@@ -199,20 +211,24 @@
     def block_of(index, start, size):
         return held.at[pl.ds(index * items + start, size)]
 
-    def ring_step(step):
-        copies = []
-        last = step == half - 1
-        for way, to in ((0, right), (1, left)):
-            shift = n_rows - step if way == 0 else step
-            owner = ring_index(lax.rem(place + shift, n_rows), n_rows)
-            size = items // 2 if last else items
-            start = items // 2 if last and way == 1 else 0
-            target = block_of(owner, start, size)
-            copies.append(remote(
-                table_ref.at[pl.ds(start, size)] if step == 0 else target,
-                target, ring_send.at[way, step], ring_recv.at[way, step], {"rows": to},
-            ))
-        return copies
+    def halves(step):
+        return range(1 if step == half - 1 else 2)
+
+    def half_start(way, part):
+        return (way + part) % 2 * (items // 2)
+
+    def ring_owner(way, step):
+        shift = n_rows - step if way == 0 else step
+        return ring_index(lax.rem(place + shift, n_rows), n_rows)
+
+    def ring_send_half(way, step, part):
+        start, size = half_start(way, part), items // 2
+        target = block_of(ring_owner(way, step), start, size)
+        return remote(
+            table_ref.at[pl.ds(start, size)] if step == 0 else target, target,
+            ring_send.at[way, 2 * step + part], ring_recv.at[way, 2 * step + part],
+            {"rows": right if way == 0 else left},
+        )
 
     outs = []
 
@@ -229,23 +245,15 @@
         block = held[pl.ds(index * items + start, size), :]
         gram_ref[...] += dot(block, block, ((0,), (0,)))
 
-    def ring_arrivals(step):
-        last = step == half - 1
-        found = []
-        for way in (0, 1):
-            shift = n_rows - step - 1 if way == 0 else step + 1
-            owner = ring_index(lax.rem(place + shift, n_rows), n_rows)
-            size = items // 2 if last else items
-            start = items // 2 if last and way == 1 else 0
-            found.append((owner, start, size))
-        return found
-
     mine_users = pl.ds(me_row * users_dev, users_dev)
     first = [
         remote(users_ref, users.at[me_dim, mine_users], first_send.at[k], first_recv.at[k], {"rows": row_peer(k)})
         for k in range(1, n_rows)
     ]
-    ring = [ring_step(0)]
+    ring = {}
+    for part in halves(0):
+        for way in (0, 1):
+            ring[way, 0, part] = ring_send_half(way, 0, part)
     table_far = [
         remote(table_ref, tables.at[me_dim], table_send.at[k], table_recv.at[k], {"dim": dim_peer(k)})
         for k in range(1, levels)
@@ -298,13 +306,15 @@
             ))
 
     for step in range(half):
-        for copy in ring[step]:
-            copy.wait_recv()
-        if step < half - 1:
-            ring.append(ring_step(step + 1))
-        for found in ring_arrivals(step):
-            keep(*found)
-            add_gram(*found)
+        for part in halves(step):
+            for way in (0, 1):
+                ring[way, step, part].wait_recv()
+                if step < half - 1 and part in halves(step + 1):
+                    ring[way, step + 1, part] = ring_send_half(way, step + 1, part)
+            for way in (0, 1):
+                found = (ring_owner(way, step + 1), half_start(way, part), items // 2)
+                keep(*found)
+                add_gram(*found)
         if step == 0:
             relay()
         if step == 1:
@@ -315,11 +325,8 @@
         sums[k - 1].wait_recv()
         times = times + arrived[k]
     times_ref[...] = times
-    for copy in first + table_far + table_near + users_far + users_near + sums + ring[0]:
+    for copy in first + table_far + table_near + users_far + users_near + sums + list(ring.values()):
         copy.wait_send()
-    for copies in ring[1:]:
-        for copy in copies:
-            copy.wait_send()
     for copy in outs:
         copy.wait()
 
@@ -345,9 +352,9 @@
             pltpu.VMEM((n_dim, n_rows * users_dev, width), BF16),
             pltpu.VMEM((n_rows * users_dev, width), F32),
             pltpu.VMEM((n_rows, users_dev, width), F32),
-            dma((2, half)),
-            dma((2, half)),
-            dma((n_rows + 1,)),
+            dma((2, 2 * half)),
+            dma((2, 2 * half)),
+            dma((2 * n_rows,)),
             dma((n_rows,)),
             dma((n_rows,)),
             dma((n_dim,)),
@@ -384,9 +391,12 @@
     live = lax.broadcasted_iota(jnp.int32, (users_dev, list_len), 1) < counts[:, None]
     picked = shard_rows[table_rows]
     fetched = jnp.where(live[..., None], picked, jnp.zeros_like(picked))
-    predicted = lax.psum(
-        jnp.einsum("ub,ujb->uj", user_rows, fetched, preferred_element_type=F32), "dim"
-    )
+    partial_value = jnp.einsum("ub,ujb->uj", user_rows, fetched, preferred_element_type=F32)
+    n_dim = lax.axis_size("dim")
+    predicted = partial_value
+    for k in range(1, n_dim):
+        pairs = [(d, (d + k) % n_dim) for d in range(n_dim)]
+        predicted = predicted + lax.ppermute(partial_value, "dim", pairs)
 
     inverse = pl.pallas_call(
         functools.partial(inverse_kernel, weight_unobs),
@@ -394,6 +404,7 @@
         in_specs=[vmem],
         out_specs=vmem,
         scratch_shapes=[pltpu.VMEM((width, width), F32)],
+        cost_estimate=pl.CostEstimate(flops=20_000_000_000, bytes_accessed=524288, transcendentals=0),
         name="inverse",
     )(diag_gram)
     return pl.pallas_call(

time: 127 us -> 103 us (0.81); the launches traced: 127 us -> 101 us
  Pallas kernels: 102 us -> 84 us
  blocking collectives: 10.5 us -> 0 us
  starting transfers between devices: 0 us -> 2.02 us
    pallas_call x1, Pallas kernels: 24.4 us -> 9.37 us  [on_device(): pl.pallas_call(functools.partial(inverse_kernel, weight_unobs), out_shape...]
    psum x1 -> x0, blocking collectives: 10.5 us -> none  [on_device(): lax.psum(jnp.einsum('ub,ujb->uj', user_rows, fetched, preferred_element_t...]
    pallas_call x1, Pallas kernels: 67.1 us -> 64.2 us  [exchange(): pl.pallas_call(functools.partial(exchange_kernel, n_rows, n_dim), out_sha...]
    ppermute x0 -> x3, starting transfers between devices: none -> 2.02 us  [on_device(): predicted = predicted + lax.ppermute(partial_value, 'dim', pairs)]
  transfers between devices with their start and end apart: 0 -> 3, of which waited for: 0 -> 0; matrix products, arithmetic and copies ran while one was open for 0% -> 1% of each run, Pallas kernels for 0% -> 9%
where the time goes in v3:
time: 103 us; the launch traced here: 101 us
  Pallas kernels  84 us (82%)
  local copies, waits for them, and re-layouts  11.4 us (11%)
  matrix products  2.43 us (2%)
  starting transfers between devices  2.02 us (2%)
  other arithmetic  1.21 us (1%)
    pallas_call x1, Pallas kernels, exchange(): pl.pallas_call(functools.partial(exchange_kernel, n_rows, n_dim), out_sha...  64.2 us
    pallas_call x1, Pallas kernels, on_device(): pl.pallas_call(functools.partial(solve_kernel, weight_unobs), out_shape=j...  10.5 us
    pallas_call x1, Pallas kernels, on_device(): pl.pallas_call(functools.partial(inverse_kernel, weight_unobs), out_shape...  9.37 us
    gather x1, local copies, waits for them, and re-layouts, on_device(): picked = shard_rows[table_rows]  9.37 us
  transfers between devices with their start and end apart: 3, of which 0 were waited for; matrix products, arithmetic and copies ran while one was open for 1% of the time, Pallas kernels for 9%

profile of v3, /device:TPU:12, one launch (start us, length us, event | category | flops | bytes accessed | tf_op | source)
XLA Modules:
  0.0 101.2 jit_solution(13495171546743822727)
XLA Ops:
  0.0 0.8 copy.6
  0.8 0.1 reshape.139
  0.9 2.0 %fusion = f32[2048]{0:T(1024)S(1)} fusion(s32[2048]{0:T(1024)S(1)} %get-tuple-element.12, s32[2048]{0:T(1024)S(1)} %get-tuple-element.11, s32[8192]{0:T(1024)} %param.9), kind=kOutput, calls=%fused_computation.2 | convolution fusion | flops 202250240 | bytes 57344 | tf_op jit(solution)/shard_map/dot_general | solution.py:30
  2.9 0.1 convert_element_type.27
  3.0 0.1 reshape.142
  3.1 0.7 fusion.12
  3.8 64.2 %exchange.1 = (bf16[8192,256]{1,0:T(8,128)(2,1)}, f32[256,256]{1,0:T(8,128)}, f32[64,256]{1,0:T(8,128)}) custom-call(bf16[1024,256]{1,0:T(8,128)(2,1)} %table_ref.1, bf16[64,256]{1,0:T(8,128)(2,1)} %own_ref.1), custom_call_target="tpu_custom_call" | custom-call | tf_op jit(solution)/shard_map/exchange/pallas_call | solution.py:340
  68.0 0.0 copy-start.1
  68.0 9.4 %gather_fusion = bf16[2048,256]{1,0:T(8,128)(2,1)S(1)} fusion(bf16[8192,256]{1,0:T(8,128)(2,1)} %get-tuple-element.8, s32[2048]{0:T(1024)S(1)} %broadcast_clamp_fusion), kind=kCustom, calls=%fused_computation | custom fusion | bytes 2105344 | tf_op jit(solution)/shard_map/gather | solution.py:392
  77.4 0.0 copy-done.1
  77.4 0.4 fusion.1
  77.8 0.1 collective-permute-start
  77.9 0.6 collective-permute-start.1
  78.5 1.4 %collective-permute-start.2 = (f32[64,32]{1,0:T(8,128)S(1)}, f32[64,32]{1,0:T(8,128)S(1)}, u32[]{:S(2)}, u32[]{:S(2)}) collective-permute-start(f32[64,32]{1,0:T(8,128)S(1)} %bitcast.13), channel_id=1, source_target_pairs={{0,24},{8,0},{16,8},{24,16},{1,25},{9,1},{17,9},{25,17},{2,26},{10... | collective-permute-start | bytes 24584 | tf_op jit(solution)/shard_map/ppermute | solution.py:399
  79.8 0.1 lt.37
  79.9 0.0 copy-start.2
  79.9 9.4 %inverse.1.inverse_ref = f32[256,256]{1,0:T(8,128)} custom-call(f32[256,256]{1,0:T(8,128)} %get-tuple-element.9.gram_ref), custom_call_target="tpu_custom_call" | custom-call | flops 20000000000 | bytes 524288 | tf_op jit(solution)/shard_map/inverse/pallas_call | solution.py:401
  89.3 0.4 broadcast_select_fusion.rows_ref
  89.7 0.0 collective-permute-done
  89.8 0.0 collective-permute-done.1
  89.8 0.0 collective-permute-done.2
  89.8 0.0 copy-done.2
  89.8 0.0 copy-start
  89.8 0.9 copy-done
  90.8 10.5 %solve.1 = f32[64,256]{1,0:T(8,128)} custom-call(bf16[2048,256]{1,0:T(8,128)(2,1)S(1)} %broadcast_select_fusion.rows_ref, f32[64,32]{1,0:T(8,128)S(1)} %get-tuple-element.13.live_ref, f32[64,32]{1,0:T(8,128)S(1)} %add_add_fusion.predicted_ref, f32[256,256]{1,0:T(8,128)S(1)} %copy-done, f32[64,256]{1,0:T(8,128)S(1)} %copy-done.2, bf16[64,256]{1,0:T(8,128)(2,1)S(1)} %copy-done.1), custom_call_target="tpu_custom_call" | custom-call | tf_op jit(solution)/shard_map/solve/pallas_call | solution.py:410
  (5 shorter events, 0.1 us)
Async XLA Ops:
  68.0 9.4 %copy-start.1 = (bf16[64,256]{1,0:T(8,128)(2,1)S(1)}, bf16[64,256]{1,0:T(8,128)(2,1)}, u32[]{:S(2)}) copy-start(bf16[64,256]{1,0:T(8,128)(2,1)} %own_ref.1) | copy-start | bytes 98308
  77.8 11.9 %collective-permute-start = (f32[64,32]{1,0:T(8,128)S(1)}, f32[64,32]{1,0:T(8,128)S(1)}, u32[]{:S(2)}, u32[]{:S(2)}) collective-permute-start(f32[64,32]{1,0:T(8,128)S(1)} %bitcast.11), channel_id=1, source_target_pairs={{0,8},{8,16},{16,24},{24,0},{1,9},{9,17},{17,25},{25,1},{2,10},{10... | collective-permute-start | bytes 24584 | tf_op jit(solution)/shard_map/ppermute | solution.py:399
  77.9 11.9 %collective-permute-start.1 = (f32[64,32]{1,0:T(8,128)S(1)}, f32[64,32]{1,0:T(8,128)S(1)}, u32[]{:S(2)}, u32[]{:S(2)}) collective-permute-start(f32[64,32]{1,0:T(8,128)S(1)} %bitcast.12), channel_id=1, source_target_pairs={{0,16},{8,24},{16,0},{24,8},{1,17},{9,25},{17,1},{25,9},{2,18},{10... | collective-permute-start | bytes 24584 | tf_op jit(solution)/shard_map/ppermute | solution.py:399
  78.5 11.3 %collective-permute-start.2 = (f32[64,32]{1,0:T(8,128)S(1)}, f32[64,32]{1,0:T(8,128)S(1)}, u32[]{:S(2)}, u32[]{:S(2)}) collective-permute-start(f32[64,32]{1,0:T(8,128)S(1)} %bitcast.13), channel_id=1, source_target_pairs={{0,24},{8,0},{16,8},{24,16},{1,25},{9,1},{17,9},{25,17},{2,26},{10... | collective-permute-start | bytes 24584 | tf_op jit(solution)/shard_map/ppermute | solution.py:399
  79.9 9.9 %copy-start.2 = (f32[64,256]{1,0:T(8,128)S(1)}, f32[64,256]{1,0:T(8,128)}, u32[]{:S(2)}) copy-start(f32[64,256]{1,0:T(8,128)} %get-tuple-element.10.times_ref) | copy-start | bytes 196612
  89.8 1.0 copy-start

commit v4 on v3

--- a/solution.py
+++ b/solution.py
@@ -246,14 +246,14 @@
         gram_ref[...] += dot(block, block, ((0,), (0,)))
 
     mine_users = pl.ds(me_row * users_dev, users_dev)
+    ring = {}
+    for part in halves(0):
+        for way in (0, 1):
+            ring[way, 0, part] = ring_send_half(way, 0, part)
     first = [
         remote(users_ref, users.at[me_dim, mine_users], first_send.at[k], first_recv.at[k], {"rows": row_peer(k)})
         for k in range(1, n_rows)
     ]
-    ring = {}
-    for part in halves(0):
-        for way in (0, 1):
-            ring[way, 0, part] = ring_send_half(way, 0, part)
     table_far = [
         remote(table_ref, tables.at[me_dim], table_send.at[k], table_recv.at[k], {"dim": dim_peer(k)})
         for k in range(1, levels)
@@ -266,13 +266,19 @@
     keep(me_row, 0, items)
     add_gram(me_row, 0, items)
 
-    for copy in first:
-        copy.wait_recv()
-    users_far = [
-        remote(users.at[me_dim], users.at[me_dim], users_send.at[k], users_recv.at[k], {"dim": dim_peer(k)})
-        for k in range(1, levels)
-    ]
-    users_near = [remote(users.at[me_dim], users.at[me_dim], users_send.at[0], users_recv.at[0], {"dim": partner})]
+    users_far, users_near = [], []
+
+    def share_users():
+        for copy in first:
+            copy.wait_recv()
+        for k in range(1, levels):
+            users_far.append(remote(
+                users.at[me_dim], users.at[me_dim], users_send.at[k], users_recv.at[k], {"dim": dim_peer(k)},
+            ))
+        users_near.append(remote(
+            users.at[me_dim], users.at[me_dim], users_send.at[0], users_recv.at[0], {"dim": partner},
+        ))
+
     sums = []
 
     def relay():
@@ -316,8 +322,10 @@
                 keep(*found)
                 add_gram(*found)
         if step == 0:
+            share_users()
+        if step == 1:
             relay()
-        if step == 1:
+        if step == 2:
             score()
 
     times = staged[mine_users, :]

time: 103 us -> 102 us (level)
  Pallas kernels: 84 us -> 82.5 us
    pallas_call x1, Pallas kernels: 64.2 us -> 62.7 us  [exchange(): pl.pallas_call(functools.partial(exchange_kernel, n_rows, n_dim), out_sha...]
where the time goes in v4:
time: 102 us; the launch traced here: 99.8 us
  Pallas kernels  82.5 us (81%)
  local copies, waits for them, and re-layouts  11.4 us (11%)
  matrix products  2.43 us (2%)
  starting transfers between devices  2.02 us (2%)
  other arithmetic  1.21 us (1%)
    pallas_call x1, Pallas kernels, exchange(): pl.pallas_call(functools.partial(exchange_kernel, n_rows, n_dim), out_sha...  62.7 us
    pallas_call x1, Pallas kernels, on_device(): pl.pallas_call(functools.partial(solve_kernel, weight_unobs), out_shape=j...  10.5 us
    pallas_call x1, Pallas kernels, on_device(): pl.pallas_call(functools.partial(inverse_kernel, weight_unobs), out_shape...  9.37 us
    gather x1, local copies, waits for them, and re-layouts, on_device(): picked = shard_rows[table_rows]  9.37 us
  transfers between devices with their start and end apart: 3, of which 0 were waited for; matrix products, arithmetic and copies ran while one was open for 1% of the time, Pallas kernels for 9%

profile of v4, /device:TPU:12, one launch (start us, length us, event | category | flops | bytes accessed | tf_op | source)
XLA Modules:
  0.0 99.8 jit_solution(9002648572174622206)
XLA Ops:
  0.0 0.8 copy.6
  0.8 0.1 reshape.139
  0.9 2.0 %fusion = f32[2048]{0:T(1024)S(1)} fusion(s32[2048]{0:T(1024)S(1)} %get-tuple-element.12, s32[2048]{0:T(1024)S(1)} %get-tuple-element.11, s32[8192]{0:T(1024)} %param.9), kind=kOutput, calls=%fused_computation.2 | convolution fusion | flops 202250240 | bytes 57344 | tf_op jit(solution)/shard_map/dot_general | solution.py:30
  2.9 0.1 convert_element_type.27
  3.0 0.1 reshape.142
  3.1 0.7 fusion.12
  3.8 62.7 %exchange.1 = (bf16[8192,256]{1,0:T(8,128)(2,1)}, f32[256,256]{1,0:T(8,128)}, f32[64,256]{1,0:T(8,128)}) custom-call(bf16[1024,256]{1,0:T(8,128)(2,1)} %table_ref.1, bf16[64,256]{1,0:T(8,128)(2,1)} %own_ref.1), custom_call_target="tpu_custom_call" | custom-call | tf_op jit(solution)/shard_map/exchange/pallas_call | solution.py:348
  66.5 0.0 copy-start.1
  66.5 9.4 %gather_fusion = bf16[2048,256]{1,0:T(8,128)(2,1)S(1)} fusion(bf16[8192,256]{1,0:T(8,128)(2,1)} %get-tuple-element.8, s32[2048]{0:T(1024)S(1)} %broadcast_clamp_fusion), kind=kCustom, calls=%fused_computation | custom fusion | bytes 2105344 | tf_op jit(solution)/shard_map/gather | solution.py:400
  75.9 0.0 copy-done.1
  75.9 0.4 fusion.1
  76.3 0.1 collective-permute-start
  76.4 0.6 collective-permute-start.1
  77.0 1.4 %collective-permute-start.2 = (f32[64,32]{1,0:T(8,128)S(1)}, f32[64,32]{1,0:T(8,128)S(1)}, u32[]{:S(2)}, u32[]{:S(2)}) collective-permute-start(f32[64,32]{1,0:T(8,128)S(1)} %bitcast.13), channel_id=1, source_target_pairs={{0,24},{8,0},{16,8},{24,16},{1,25},{9,1},{17,9},{25,17},{2,26},{10... | collective-permute-start | bytes 24584 | tf_op jit(solution)/shard_map/ppermute | solution.py:407
  78.4 0.1 lt.37
  78.5 0.0 copy-start.2
  78.5 9.4 %inverse.1.inverse_ref = f32[256,256]{1,0:T(8,128)} custom-call(f32[256,256]{1,0:T(8,128)} %get-tuple-element.9.gram_ref), custom_call_target="tpu_custom_call" | custom-call | flops 20000000000 | bytes 524288 | tf_op jit(solution)/shard_map/inverse/pallas_call | solution.py:409
  87.8 0.4 broadcast_select_fusion.rows_ref
  88.3 0.0 collective-permute-done
  88.3 0.0 collective-permute-done.1
  88.3 0.0 collective-permute-done.2
  88.3 0.0 copy-done.2
  88.3 0.0 copy-start
  88.3 0.9 copy-done
  89.3 10.5 %solve.1 = f32[64,256]{1,0:T(8,128)} custom-call(bf16[2048,256]{1,0:T(8,128)(2,1)S(1)} %broadcast_select_fusion.rows_ref, f32[64,32]{1,0:T(8,128)S(1)} %get-tuple-element.13.live_ref, f32[64,32]{1,0:T(8,128)S(1)} %add_add_fusion.predicted_ref, f32[256,256]{1,0:T(8,128)S(1)} %copy-done, f32[64,256]{1,0:T(8,128)S(1)} %copy-done.2, bf16[64,256]{1,0:T(8,128)(2,1)S(1)} %copy-done.1), custom_call_target="tpu_custom_call" | custom-call | tf_op jit(solution)/shard_map/solve/pallas_call | solution.py:418
  (5 shorter events, 0.1 us)
Async XLA Ops:
  66.5 9.4 %copy-start.1 = (bf16[64,256]{1,0:T(8,128)(2,1)S(1)}, bf16[64,256]{1,0:T(8,128)(2,1)}, u32[]{:S(2)}) copy-start(bf16[64,256]{1,0:T(8,128)(2,1)} %own_ref.1) | copy-start | bytes 98308
  76.3 11.9 %collective-permute-start = (f32[64,32]{1,0:T(8,128)S(1)}, f32[64,32]{1,0:T(8,128)S(1)}, u32[]{:S(2)}, u32[]{:S(2)}) collective-permute-start(f32[64,32]{1,0:T(8,128)S(1)} %bitcast.11), channel_id=1, source_target_pairs={{0,8},{8,16},{16,24},{24,0},{1,9},{9,17},{17,25},{25,1},{2,10},{10... | collective-permute-start | bytes 24584 | tf_op jit(solution)/shard_map/ppermute | solution.py:407
  76.4 11.9 %collective-permute-start.1 = (f32[64,32]{1,0:T(8,128)S(1)}, f32[64,32]{1,0:T(8,128)S(1)}, u32[]{:S(2)}, u32[]{:S(2)}) collective-permute-start(f32[64,32]{1,0:T(8,128)S(1)} %bitcast.12), channel_id=1, source_target_pairs={{0,16},{8,24},{16,0},{24,8},{1,17},{9,25},{17,1},{25,9},{2,18},{10... | collective-permute-start | bytes 24584 | tf_op jit(solution)/shard_map/ppermute | solution.py:407
  77.0 11.3 %collective-permute-start.2 = (f32[64,32]{1,0:T(8,128)S(1)}, f32[64,32]{1,0:T(8,128)S(1)}, u32[]{:S(2)}, u32[]{:S(2)}) collective-permute-start(f32[64,32]{1,0:T(8,128)S(1)} %bitcast.13), channel_id=1, source_target_pairs={{0,24},{8,0},{16,8},{24,16},{1,25},{9,1},{17,9},{25,17},{2,26},{10... | collective-permute-start | bytes 24584 | tf_op jit(solution)/shard_map/ppermute | solution.py:407
  78.5 9.9 %copy-start.2 = (f32[64,256]{1,0:T(8,128)S(1)}, f32[64,256]{1,0:T(8,128)}, u32[]{:S(2)}) copy-start(f32[64,256]{1,0:T(8,128)} %get-tuple-element.10.times_ref) | copy-start | bytes 196612
  88.3 1.0 copy-start
